TPU v7x, 256 devices: a whole 4x4x8 slice. The times are simulated.
256 devices in a mesh: aux: 8 (over z_hi, core), row: 8 (over z_lo, y), col: 4 (over x).
Axes of the slice: x: 4, y: 4, z: 8 (z_hi: 4, z_lo: 2; z = z_hi * 2 + z_lo), core: 2. Of those that a mesh axis runs over, the one named last changes fastest.
Arguments:
- act_slab: bfloat16 [30, 1024, 4096], P(None, 'row', ('aux', 'col')), may hold values from -2 to 2
- core_slab: bfloat16 [128, 1024, 4096], P(None, 'col', ('aux', 'row')), may hold values from -2 to 2
- rotation: float32 [30, 30], replicated, may hold values from -1 to 1
- core_block: int32 [1], replicated, may hold values from 0 to 31
- core_energy: float32 [128], replicated, may hold values from -30 to -6
- vir_energy: float32 [1024], replicated, may hold values from 0.5 to 8
- act_energy: float32 [30], replicated, may hold values from -3 to 3
- rdm_two: float32 [30, 30, 30, 30], replicated, may hold values from -6 to 6
Outputs:
- amp_one: float32 [1024, 30, 4, 1024], P(('row', 'aux'), None, None, 'col')
- amp_two: float32 [1024, 30, 4, 1024], P(('row', 'aux'), None, None, 'col')
- pair_energy: float32 [2, 4, 1024], P(None, None, ('row', 'aux'))
All inputs are finite; a program needn't handle non-finite values.
Results may differ from a plain program's by a relative error of at most 0.0029.
Values may be sent and summed in bfloat16 or wider, within the bound.
A program may use at most 128 MiB of HBM per device.

v0:
```python
import jax
import jax.numpy as jnp
from jax import lax
from jax.sharding import PartitionSpec as P

NBLK = 32


def shards(act_slab, core_slab, rotation, core_block, core_energy, vir_energy, act_energy, rdm_two):
    highest = lax.Precision.HIGHEST
    block_size = core_slab.shape[0] // NBLK
    half_act = jnp.einsum(
        "st,sap->tap", rotation, act_slab.astype(jnp.float32), precision=highest
    ).astype(jnp.bfloat16)
    first_core = core_block[0] * block_size
    core_rows = lax.dynamic_slice_in_dim(core_slab, first_core, block_size, 0)
    core_levels = lax.dynamic_slice_in_dim(core_energy, first_core, block_size, 0)
    group_act = lax.all_gather(half_act, "col", axis=2, tiled=True)
    tile_rows = group_act.shape[1] // lax.axis_size("aux")
    all_core = lax.all_gather(core_rows, ("aux", "row"), axis=2, tiled=True)
    tiles = jnp.einsum(
        "tap,ibp->atib",
        lax.all_to_all(group_act, "aux", split_axis=1, concat_axis=2, tiled=True),
        all_core,
        preferred_element_type=jnp.float32,
    )
    row_start = lax.axis_index("row") * group_act.shape[1] + lax.axis_index("aux") * tile_rows
    col_start = lax.axis_index("col") * tiles.shape[3]
    vir_rows = lax.dynamic_slice_in_dim(vir_energy, row_start, tiles.shape[0], 0)
    vir_cols = lax.dynamic_slice_in_dim(vir_energy, col_start, tiles.shape[3], 0)
    trace_one = jnp.einsum("uvtv->ut", rdm_two)
    trace_two = jnp.einsum("uvvt->ut", rdm_two)
    denominator = (
        vir_rows[:, None, None, None]
        + act_energy[None, :, None, None]
        - core_levels[None, None, :, None]
        + vir_cols[None, None, None, :]
    )
    amp_one = -jnp.einsum("ut,atib->auib", trace_one, tiles, precision=highest) / denominator
    amp_two = -jnp.einsum("ut,atib->auib", trace_two, tiles, precision=highest) / denominator
    local_one = jnp.sum(amp_one * tiles, axis=(1, 3)).T
    local_two = jnp.sum(amp_two * tiles, axis=(1, 3)).T
    pair_energy = lax.psum(jnp.stack([local_one, local_two]), "col")
    return (amp_one, amp_two, pair_energy)


def solution(mesh):
    in_specs = (
        P(None, "row", ("aux", "col")),
        P(None, "col", ("aux", "row")),
        P(),
        P(),
        P(),
        P(),
        P(),
        P(),
    )
    out_specs = (
        P(("row", "aux"), None, None, "col"),
        P(("row", "aux"), None, None, "col"),
        P(None, None, ("row", "aux")),
    )
    return jax.shard_map(shards, mesh=mesh, in_specs=in_specs, out_specs=out_specs, check_vma=False)
```

profile of v0, /device:TPU:105, one launch (start us, length us, event | category | flops | bytes accessed | tf_op | source)
XLA Modules:
  0.0 372.9 jit_solution(1154443009382793167)
XLA Ops:
  7.2 0.0 copy-start
  7.2 0.0 all-gather.5.cloned.1.call-start
  7.2 1.1 copy-done
  8.4 2.9 convolution_convert_fusion
  11.3 0.0 all-gather.5.cloned.1.call-update
  11.3 0.0 all-gather.3.cloned.1.call-start
  12.0 1.6 constant_dynamic-slice_fusion
  13.6 0.0 all-gather.3.cloned.1.call-update
  13.6 0.0 copy-start.2
  13.6 0.0 copy-start.1
  13.7 53.3 %all-gather.5.cloned.1.call-done = bf16[30,128,512]{2,0,1:T(8,128)(2,1)} async-done(((bf16[30,128,128]{2,0,1:T(8,128)(2,1)}), bf16[30,128,512]{2,0,1:T(8,128)(2,1)}) %all-gather.5.cloned.1.call-update) | async-done | bytes 3932176 | tf_op jit(solution)/shard_map/all_gather | solution.py:18
  66.9 7.7 %all-to-all-start = ((bf16[30,128,512]{2,0,1:T(8,128)(2,1)}), bf16[30,128,512]{2,0,1:T(8,128)(2,1)}, u32[]{:S(2)}, u32[]{:S(2)}) async-start(bf16[30,128,512]{2,0,1:T(8,128)(2,1)} %all-gather.5.cloned.1.call-done), calls=%async_computation | async-start | bytes 8388608 | tf_op jit(solution)/shard_map/all_to_all | solution.py:23
  74.6 0.0 copy-done.2
  74.6 0.1 dynamic_slice.14
  74.7 0.8 dynamic_slice.15
  75.4 0.8 dynamic_slice.13
  76.2 0.0 copy-done.1
  76.2 0.1 broadcast_add_fusion
  76.3 0.1 broadcast_subtract_fusion
  76.4 11.8 %select_reduce_fusion = (f32[30,30]{1,0:T(8,128)S(1)}, f32[30,30]{1,0:T(8,128)S(1)}) fusion(f32[30,30,30,30]{3,2,1,0:T(8,128)} %param.15, pred[30,30]{1,0:T(8,128)(4,1)S(1)} %iota_compare_fusion), kind=kLoop, calls=%fused_computation | loop fusion | flops 3238200 | bytes 3248100 | tf_op jit(solution)/shard_map/uvvt->ut/reduce_sum | solution.py:32
  88.1 82.3 %all-to-all-done = bf16[30,128,512]{2,0,1:T(8,128)(2,1)} async-done(((bf16[30,128,512]{2,0,1:T(8,128)(2,1)}), bf16[30,128,512]{2,0,1:T(8,128)(2,1)}, u32[]{:S(2)}, u32[]{:S(2)}) %all-to-all-start) | async-done | bytes 3932192 | tf_op jit(solution)/shard_map/all_to_all | solution.py:23
  170.4 6.3 %copy.64 = bf16[30,8,16,512]{3,1,2,0:T(8,128)(2,1)} copy(bf16[30,8,16,512]{3,0,2,1:T(8,128)(2,1)} %bitcast.4) | data formatting | bytes 7864320 | tf_op jit(solution)/shard_map/all_to_all | solution.py:23
  176.7 7.1 %all_to_all.16 = bf16[30,16,4096]{2,1,0:T(8,128)(2,1)} reshape(bf16[30,16,8,512]{3,2,1,0:T(8,128)(2,1)} %bitcast.46) | data formatting | bytes 7864320 | tf_op jit(solution)/shard_map/all_to_all | solution.py:23
  183.8 149.9 %all-gather.3.cloned.1.call-done = bf16[4,256,4096]{1,2,0:T(8,128)(2,1)} async-done(((bf16[4,256,64]{1,2,0:T(8,128)(2,1)}), bf16[4,256,4096]{1,2,0:T(8,128)(2,1)}) %all-gather.3.cloned.1.call-update) | async-done | bytes 8388624 | tf_op jit(solution)/shard_map/all_gather | solution.py:20
  333.8 8.0 %fusion.7 = f32[16,30,4,256]{3,0,1,2:T(8,128)S(1)} fusion(bf16[30,16,4096]{2,1,0:T(8,128)(2,1)} %all_to_all.16, bf16[4,256,4096]{1,2,0:T(8,128)(2,1)} %all-gather.3.cloned.1.call-done), kind=kOutput, calls=%fused_computation.16 | convolution fusion | flops 4026531840 | bytes 14286848 | tf_op jit(solution)/shard_map/tap,ibp->atib/dot_general | solution.py:21
  341.8 3.7 fusion.3
  345.4 3.7 fusion.5
  349.1 2.8 multiply_reduce_fusion.1
  351.9 2.5 copy.39
  354.4 2.5 copy.40
  357.0 9.0 %psum.7 = f32[2,4,16]{2,1,0:T(4,128)} all-reduce(f32[2,4,16]{2,1,0:T(4,128)S(1)} %pad_maximum_fusion), channel_id=1, replica_groups=mesh['aux'=8,'row'=8,'col'=4] {'col'}, use_global_device_ids=true, to_apply=%region_4.0 | all-reduce | flops 128 | bytes 1024 | tf_op jit(solution)/shard_map/psum | solution.py:43
  (2 shorter events, 0.0 us)
Async XLA Ops:
  7.2 1.2 copy-start
  7.2 59.8 %all-gather.5.cloned.1.call-start = ((), (), s32[]{:S(2)}) async-start(), calls=%async_computation.2 | async-start | bytes 5242880 | tf_op jit(solution)/shard_map/all_gather | solution.py:18
  11.3 322.4 %all-gather.3.cloned.1.call-start = ((), (), s32[]{:S(2)}) async-start(), calls=%async_computation.1 | async-start | bytes 8519680 | tf_op jit(solution)/shard_map/all_gather | solution.py:20
  13.6 61.0 %copy-start.2 = (f32[128]{0:T(128)S(1)}, f32[128]{0:T(128)}, u32[]{:S(2)}) copy-start(f32[128]{0:T(128)} %param.12) | copy-start | bytes 1540
  13.6 62.6 %copy-start.1 = (f32[30]{0:T(128)S(1)}, f32[30]{0:T(128)}, u32[]{:S(2)}) copy-start(f32[30]{0:T(128)} %param.14) | copy-start | bytes 364
  66.9 103.5 %all-to-all-start = ((bf16[30,128,512]{2,0,1:T(8,128)(2,1)}), bf16[30,128,512]{2,0,1:T(8,128)(2,1)}, u32[]{:S(2)}, u32[]{:S(2)}) async-start(bf16[30,128,512]{2,0,1:T(8,128)(2,1)} %all-gather.5.cloned.1.call-done), calls=%async_computation | async-start | bytes 8388608 | tf_op jit(solution)/shard_map/all_to_all | solution.py:23
Sparse Core Ops, SparseCore 0:
  11.5 55.4 all-gather.4
  69.3 264.3 all-gather.2
where the time goes:
time: 373 us
  waiting for transfers between devices  286 us (77%)
  local copies, waits for them, and re-layouts  22.8 us (6%)
  matrix products  18.3 us (5%)
  between operations  14.8 us (4%)
  other arithmetic  14.7 us (4%)
  blocking collectives  9.03 us (2%)
  starting transfers between devices  7.75 us (2%)
    all_gather x1, waiting for transfers between devices, shards(): all_core = lax.all_gather(core_rows, ('aux', 'row'), axis=2, tiled=True)  150 us
    all_to_all x1, waiting for transfers between devices, shards(): lax.all_to_all(group_act, 'aux', split_axis=1, concat_axis=2, tiled=True)  82.3 us
    all_gather x1, waiting for transfers between devices, shards(): group_act = lax.all_gather(half_act, 'col', axis=2, tiled=True)  53.3 us
    all_to_all x2, local copies, waits for them, and re-layouts, shards(): lax.all_to_all(group_act, 'aux', split_axis=1, concat_axis=2, tiled=True)  13.4 us
    reduce_sum x1, other arithmetic, shards(): trace_two = jnp.einsum('uvvt->ut', rdm_two)  11.8 us
    psum x1, blocking collectives, shards(): pair_energy = lax.psum(jnp.stack([local_one, local_two]), 'col')  9.03 us
    dot_general x1, matrix products, shards(): jnp.einsum('tap,ibp->atib', lax.all_to_all(group_act, 'aux', split_axis=1...  8 us
    all_to_all x1, starting transfers between devices, shards(): lax.all_to_all(group_act, 'aux', split_axis=1, concat_axis=2, tiled=True)  7.67 us
  transfers between devices with their start and end apart: 3, of which 3 were waited for; matrix products, arithmetic and copies ran while one was open for 6% of the time, Pallas kernels for 0%

commit v1 on v0

v1 whole, which is shorter than its diff:
```python
import functools

import jax
import jax.numpy as jnp
from jax import lax
from jax.experimental import pallas as pl
from jax.experimental.pallas import tpu as pltpu
from jax.sharding import PartitionSpec as P

NBLK = 32
F32 = jnp.float32
BF16 = jnp.bfloat16
HIGH = lax.Precision.HIGHEST
NT = (((1,), (1,)), ((), ()))

ORDER = (
    ("A", 0, 0, 1), ("T", 0),
    ("C", -1, 0, 0), ("C", 1, 0, 0), ("A", -1, 0, 0), ("A", 1, 0, 0),
    ("A", 1, 0, 1), ("A", -1, 0, 1), ("T", 1), ("C", 2, 0, 0), ("T", 2),
    ("A", 0, -1, 0), ("A", 0, 1, 0), ("C", 0, -1, 0), ("C", 0, 1, 0), ("T", 3), ("T", 4),
    ("A", -1, -1, 0), ("A", -1, 1, 0), ("A", 1, -1, 0), ("A", 1, 1, 0),
    ("C", -1, -1, 0), ("C", -1, 1, 0), ("C", 1, -1, 0), ("C", 1, 1, 0),
    ("A", 0, -1, 1), ("A", 0, 1, 1), ("C", 0, -2, 0), ("C", 0, 2, 0), ("G",),
    ("A", -1, -1, 1), ("A", -1, 1, 1), ("C", -1, -2, 0), ("C", -1, 2, 0),
    ("C", 2, -1, 0), ("C", 2, 1, 0), ("A", 0, 2, 0), ("A", 1, -1, 1), ("A", 1, 1, 1),
    ("C", 0, -3, 0), ("C", 0, 3, 0), ("C", 1, -2, 0), ("C", 1, 2, 0), ("A", 1, 2, 0),
    ("M", 0, 0), ("C", 0, 4, 0), ("A", -1, 2, 0), ("A", 0, 2, 1), ("M", 0, 1),
    ("C", 1, -3, 0), ("C", 1, 3, 0), ("C", 2, -2, 0), ("C", 2, 2, 0),
    ("A", 1, 2, 1), ("C", -1, -3, 0), ("C", -1, 3, 0), ("A", -1, 2, 1),
    ("C", -1, 4, 0), ("C", 1, 4, 0), ("C", 2, -3, 0), ("C", 2, 3, 0),
    ("M", 1, 0), ("M", -1, 0), ("C", 2, 4, 0), ("M", 1, 1), ("M", -1, 1),
    ("M", 2, 0), ("M", 2, 1),
)


def kernel(
    act, core, rdm, rot, block, levels, vir, occ,
    one, two, energy,
    abuf, cbuf, acc, rdmv, amp, mix, tr, ebuf,
    send_sem, recv_a, recv_c, recv_h, recv_e, local_sem, out_sem,
):
    nact = act.shape[0]
    sub = abuf.shape[3]
    aux, row, col = lax.axis_index("aux"), lax.axis_index("row"), lax.axis_index("col")
    h, c = aux // 2, aux % 2
    z, y = h * 2 + row // 4, row % 4

    def device(dx=0, dy=0, dz=0, dc=0):
        zz = (z + dz + 8) % 8
        return (
            (zz // 2) * 2 + (c + dc) % 2,
            (zz % 2) * 4 + (y + dy + 4) % 4,
            (col + dx + 4) % 4,
        )

    def act_slot(dx, dh, dc):
        return (col + dx + 4) % 4, ((h + dh + 4) % 4) * 2 + (c + dc) % 2

    def core_slot(dy, dz, dc):
        a, r, _ = device(dy=dy, dz=dz, dc=dc)
        return a, r

    local = [
        pltpu.make_async_copy(rdm, rdmv, local_sem.at[0]),
        pltpu.make_async_copy(
            act.at[:, pl.ds(pl.multiple_of(aux * sub, sub), sub), :], abuf.at[col, aux], local_sem.at[1]
        ),
        pltpu.make_async_copy(core, cbuf.at[aux, row], local_sem.at[2]),
    ]
    for copy in local:
        copy.start()

    partners = [device(dz=2 * dh, dc=dc) for dh in range(4) for dc in range(2) if (dh, dc) != (0, 0)]
    partners += [device(dx=dx) for dx in (1, -1, 2)]
    partners += [device(dy=dy) for dy in (1, -1)]
    partners += [device(dz=dz) for dz in (1, -1)]
    barrier = pltpu.get_barrier_semaphore()
    for partner in partners:
        pl.semaphore_signal(barrier, inc=1, device_id=partner, device_id_type=pl.DeviceIdType.MESH)
    pl.semaphore_wait(barrier, len(partners))

    sends = []

    def send(src, dst, sem, target):
        copy = pltpu.make_async_remote_copy(
            src_ref=src, dst_ref=dst, send_sem=send_sem.at[len(sends)], recv_sem=sem,
            device_id=target, device_id_type=pl.DeviceIdType.MESH,
        )
        copy.start()
        sends.append(copy)

    def arrived(dst, sem):
        pltpu.make_async_remote_copy(
            src_ref=dst, dst_ref=dst, send_sem=send_sem.at[0], recv_sem=sem,
            device_id=device(dc=1), device_id_type=pl.DeviceIdType.MESH,
        ).wait_recv()

    def scatter_act(dh, dc):
        target = device(dz=2 * dh, dc=dc)
        rows = pl.ds(pl.multiple_of(target[0] * sub, sub), sub)
        send(act.at[:, rows, :], abuf.at[col, aux], recv_a.at[col * 8 + aux], target)

    def pass_act(dx, dh, dc, to):
        x, j = act_slot(dx, dh, dc)
        send(abuf.at[x, j], abuf.at[x, j], recv_a.at[x * 8 + j], device(dx=to))

    def pass_core(from_y, from_z, **to):
        a, r = core_slot(from_y, from_z, 0)
        send(cbuf.at[a, r], cbuf.at[a, r], recv_c.at[a * 8 + r], device(**to))

    def half_core(dz, half, to):
        a, r = core_slot(0, dz, 0)
        sem = recv_h.at[0] if half else recv_c.at[a * 8 + r]
        part = cbuf.at[a, r, pl.ds(2 * half, 2)]
        send(part, part, sem, device(dz=to))

    def on_act(dx, dh, dc):
        if dx == 0 and (dh, dc) != (0, 0):
            pass_act(0, dh, dc, 1)
            pass_act(0, dh, dc, -1)
        if dx == -1 and (dh + dc) % 2 == 0:
            pass_act(-1, dh, dc, 1)
        if dx == 1 and (dh + dc) % 2 == 1:
            pass_act(1, dh, dc, -1)
        if (dx, dh, dc) == (0, 1, 0):
            scatter_act(1, 1)
            scatter_act(-1, 1)
        if (dx, dh, dc) == (0, 1, 1):
            scatter_act(2, 0)
        if (dx, dh, dc) == (0, 2, 0):
            scatter_act(2, 1)

    def on_core(dy, dz):
        if dy == 0:
            if -2 <= dz < 0:
                pass_core(0, dz, dz=1)
            if 0 < dz <= 2:
                pass_core(0, dz, dz=-1)
            if dz == -3:
                half_core(dz, 0, 1)
            if dz == 3:
                half_core(dz, 1, -1)
            pass_core(0, dz, dy=1)
            pass_core(0, dz, dy=-1)
        if dy == -1 and dz % 2 == 0:
            pass_core(-1, dz, dy=1)
        if dy == 1 and dz % 2 == 1:
            pass_core(1, dz, dy=-1)
        pass_core(dy, dz, dc=1)

    scatter_act(1, 0)
    scatter_act(-1, 0)
    mine = act.at[:, pl.ds(pl.multiple_of(aux * sub, sub), sub), :]
    for to in (1, -1):
        send(mine, abuf.at[col, aux], recv_a.at[col * 8 + aux], device(dx=to))
    for to in (dict(dz=1), dict(dz=-1), dict(dy=1), dict(dy=-1), dict(dc=1)):
        send(core, cbuf.at[aux, row], recv_c.at[aux * 8 + row], device(**to))
    scatter_act(0, 1)

    def trace_step(u, carry):
        by_lane = jnp.zeros((nact, nact), F32)
        by_row = jnp.zeros((nact, nact), F32)
        lanes = lax.broadcasted_iota(jnp.int32, (nact, nact), 1)
        rows = lax.broadcasted_iota(jnp.int32, (nact, nact), 0)
        for v in range(nact):
            piece = rdmv[u, v]
            by_lane = jnp.where(lanes == v, piece, by_lane)
            by_row = jnp.where(rows == v, piece, by_row)
        first = jnp.sum(by_lane, axis=1, keepdims=True)
        second = jnp.sum(by_row, axis=0, keepdims=True)
        tr[0] = jnp.where(lanes == u, first, tr[0])
        tr[1] = jnp.where(rows == u, second, tr[1])
        return carry

    def build_mix():
        eye = (
            lax.broadcasted_iota(jnp.int32, (nact, nact), 0) == lax.broadcasted_iota(jnp.int32, (nact, nact), 1)
        ).astype(F32)
        spread = (
            lax.broadcasted_iota(jnp.int32, (256, nact), 0) // 8 == lax.broadcasted_iota(jnp.int32, (256, nact), 1)
        ).astype(F32)
        same = (
            lax.broadcasted_iota(jnp.int32, (8 * nact, 256), 0) % 8
            == lax.broadcasted_iota(jnp.int32, (8 * nact, 256), 1) % 8
        )

        def nt(a, b):
            return lax.dot_general(a, b, NT, precision=HIGH, preferred_element_type=F32)

        turn = rot[...]
        for k, small in enumerate((nt(nt(eye, tr[0]), turn), nt(tr[1], turn), nt(eye, turn))):
            tall = jnp.dot(spread[: 8 * nact], small, precision=HIGH, preferred_element_type=F32)
            full = jnp.where(same, nt(tall, spread), 0.0)
            high = full.astype(BF16)
            low = (full - high.astype(F32)).astype(BF16)
            at = pl.ds(k * 8 * nact, 8 * nact)
            mix[at, 0:256] = high
            mix[at, 256:512] = low
            mix[at, 512:768] = high

    done = []

    def product(dh, dc):
        j = ((h + dh + 4) % 4) * 2 + (c + dc) % 2
        left = jnp.concatenate(
            [abuf[x, j].reshape(nact * sub, abuf.shape[4]) for x in range(4)], axis=1
        )
        first = not done
        done.append(j)

        def step(i, carry):
            right = cbuf[j, :, i].reshape(left.shape[1], cbuf.shape[4])
            out = jnp.dot(left, right, preferred_element_type=F32).reshape(acc.shape[1:])
            acc[i] = out if first else acc[i] + out
            return carry

        lax.fori_loop(0, 4, step, 0)

    waited = set()

    def take_core(dy, dz, dc):
        if (dy, dz, dc) in waited or (dy, dz, dc) == (0, 0, 0):
            return
        waited.add((dy, dz, dc))
        a, r = core_slot(dy, dz, dc)
        if (dy, dz, dc) == (0, 4, 0):
            arrived(cbuf.at[a, r, pl.ds(0, 2)], recv_c.at[a * 8 + r])
            arrived(cbuf.at[a, r, pl.ds(2, 2)], recv_h.at[0])
        else:
            arrived(cbuf.at[a, r], recv_c.at[a * 8 + r])

    for event in ORDER:
        kind = event[0]
        if kind == "A":
            x, j = act_slot(*event[1:])
            arrived(abuf.at[x, j], recv_a.at[x * 8 + j])
            on_act(*event[1:])
        elif kind == "C":
            take_core(*event[1:])
            on_core(event[1], event[2])
        elif kind == "T":
            part = event[1]
            if part == 0:
                local[0].wait()
                tr[...] = jnp.zeros_like(tr)
            lax.fori_loop(part * nact // 5, (part + 1) * nact // 5, trace_step, 0)
        elif kind == "G":
            build_mix()
        else:
            _, dh, dc = event
            if not done:
                local[1].wait()
                local[2].wait()
            x, j = act_slot(2, dh, dc)
            arrived(abuf.at[x, j], recv_a.at[x * 8 + j])
            for dz in (2 * dh - 1, 2 * dh, 2 * dh + 1):
                dz = (dz + 3) % 8 - 3
                for dy in (0, 1, -1, 2):
                    take_core(dy, dz, dc)
            product(dh, dc)

    ebuf[col] = jnp.zeros(ebuf.shape[1:], F32)
    lanes = lax.broadcasted_iota(jnp.int32, (8 * nact, 128), 1)
    rows = lax.broadcasted_iota(jnp.int32, (8 * nact, 128), 0)
    vir_row = vir[pl.ds((row * 128 + aux * sub) // 128, 1), :]
    by_occ = jnp.sum(jnp.where(lanes == rows // 8, occ[...], 0.0), axis=1, keepdims=True)
    by_col = jnp.concatenate([vir[pl.ds(2 * col, 1), :], vir[pl.ds(2 * col + 1, 1), :]], axis=1)
    by_row = [
        jnp.sum(jnp.where(lanes == aux * sub + g * 8 + rows % 8, vir_row, 0.0), axis=1, keepdims=True) + by_occ
        for g in range(2)
    ]
    first_core = block[0] * 4
    slots = lax.broadcasted_iota(jnp.int32, (8, 128), 1)

    def finish(i, carry):
        level = levels[first_core + i]
        for g in range(2):
            at = pl.ds(8 * g, 8)
            tile = acc[i, :, at, :].reshape(8 * nact, acc.shape[3])
            high = tile.astype(BF16)
            low = (tile - high.astype(F32)).astype(BF16)
            pad = jnp.zeros((256 - 8 * nact, acc.shape[3]), BF16)
            right = jnp.concatenate([high, pad, high, pad, low, pad], axis=0)
            mixed = jnp.dot(mix[...], right, preferred_element_type=F32)
            scale = -1.0 / ((by_row[g] - level) + by_col)
            turned = mixed[16 * nact :]
            for k in range(2):
                value = mixed[8 * nact * k : 8 * nact * (k + 1)] * scale
                amp[k, i, :, at, :] = value.reshape(nact, 8, acc.shape[3])
                part = jnp.sum((value * turned).reshape(nact, 8, acc.shape[3]), axis=0)
                part = jnp.sum(part, axis=1, keepdims=True)
                ebuf[col, at, :] = ebuf[col, at, :] + jnp.where(slots == k * 4 + i, part, 0.0)
        for k, out in enumerate((one, two)):
            pltpu.make_async_copy(amp.at[k, i], out.at[i], out_sem.at[k, i]).start()
        return carry

    lax.fori_loop(0, 4, finish, 0)
    for dx in (1, -1, 2):
        send(ebuf.at[col], ebuf.at[col], recv_e.at[col], device(dx=dx))
    for dx in (1, -1, 2):
        x = (col + dx + 4) % 4
        arrived(ebuf.at[x], recv_e.at[x])
    total = ((ebuf[0] + ebuf[1]) + ebuf[2]) + ebuf[3]
    energy[...] = total.T[:8]
    for copy in sends:
        copy.wait_send()
    for i in range(4):
        for k, out in enumerate((one, two)):
            pltpu.make_async_copy(amp.at[k, i], out.at[i], out_sem.at[k, i]).wait()


def shards(act_slab, core_slab, rotation, core_block, core_energy, vir_energy, act_energy, rdm_two):
    block_size = core_slab.shape[0] // NBLK
    nact, tile, depth = act_slab.shape
    sub = tile // lax.axis_size("aux")
    cols, core_depth = core_slab.shape[1:]
    core_rows = lax.dynamic_slice_in_dim(core_slab, core_block[0] * block_size, block_size, 0)
    core_rows = jnp.transpose(core_rows, (0, 2, 1))
    any_space = pl.BlockSpec(memory_space=pl.ANY)
    vmem = pl.BlockSpec(memory_space=pltpu.VMEM)
    smem = pl.BlockSpec(memory_space=pltpu.SMEM)
    out = jax.ShapeDtypeStruct((block_size, nact, sub, cols), F32)
    occ = jnp.pad(act_energy, (0, 128 - nact)).reshape(1, 128)
    one, two, energy = pl.pallas_call(
        kernel,
        out_shape=(out, out, jax.ShapeDtypeStruct((2 * block_size, sub), F32)),
        in_specs=[any_space, any_space, any_space, vmem, smem, smem, vmem, vmem],
        out_specs=(any_space, any_space, vmem),
        scratch_shapes=[
            pltpu.VMEM((4, 8, nact, sub, depth), BF16),
            pltpu.VMEM((8, 8, block_size, core_depth, cols), BF16),
            pltpu.VMEM((block_size, nact, sub, cols), F32),
            pltpu.VMEM(rdm_two.shape, F32),
            pltpu.VMEM((2, block_size, nact, sub, cols), F32),
            pltpu.VMEM((3 * 8 * nact, 768), BF16),
            pltpu.VMEM((2, nact, nact), F32),
            pltpu.VMEM((4, sub, 128), F32),
            pltpu.SemaphoreType.DMA((98,)),
            pltpu.SemaphoreType.DMA((32,)),
            pltpu.SemaphoreType.DMA((64,)),
            pltpu.SemaphoreType.DMA((1,)),
            pltpu.SemaphoreType.DMA((4,)),
            pltpu.SemaphoreType.DMA((3,)),
            pltpu.SemaphoreType.DMA((2, 4)),
        ],
        compiler_params=pltpu.CompilerParams(
            collective_id=0, has_side_effects=True, vmem_limit_bytes=56 * 2**20
        ),
    )(act_slab, core_rows, rdm_two, rotation, core_block, core_energy, vir_energy.reshape(8, 128), occ)
    return (
        jnp.transpose(one, (2, 1, 0, 3)),
        jnp.transpose(two, (2, 1, 0, 3)),
        energy.reshape(2, block_size, sub),
    )


def solution(mesh):
    in_specs = (
        P(None, "row", ("aux", "col")),
        P(None, "col", ("aux", "row")),
        P(),
        P(),
        P(),
        P(),
        P(),
        P(),
    )
    out_specs = (
        P(("row", "aux"), None, None, "col"),
        P(("row", "aux"), None, None, "col"),
        P(None, None, ("row", "aux")),
    )
    return jax.shard_map(shards, mesh=mesh, in_specs=in_specs, out_specs=out_specs, check_vma=False)
```

time: 373 us -> 85.7 us (0.23)
  the two profiles are of different devices: /device:TPU:105 before, /device:TPU:1 now
where the time goes in v1:
time: 85.7 us; the launch traced here: 85.5 us
  Pallas kernels  74.2 us (87%)
  local copies, waits for them, and re-layouts  10.1 us (12%)
  between operations  1.3 us (2%)
    pallas_call x1, Pallas kernels, shards(): pl.pallas_call(kernel, out_shape=(out, out, jax.ShapeDtypeStruct((2 * blo...  74.2 us
    unnamed x7, local copies, waits for them, and re-layouts  7.36 us

profile of v1, /device:TPU:1, one launch (start us, length us, event | category | flops | bytes accessed | tf_op | source)
XLA Modules:
  0.0 85.5 jit_solution(2225550514524215712)
XLA Ops:
  1.3 1.2 %pad_bitcast_fusion.occ = f32[1,128]{1,0:T(1,128)} fusion(f32[30]{0:T(128)} %param.14), kind=kLoop, calls=%fused_computation.1 | loop fusion | bytes 632 | tf_op jit(solution)/shard_map/reshape | solution.py:323
  2.5 1.6 %dynamic-slice_bitcast_fusion.core = bf16[4,64,256]{2,1,0:T(8,128)(2,1)} fusion(bf16[128,256,64]{1,2,0:T(8,128)(2,1)} %param.9, s32[]{:T(128)S(6)} %select_n.3), kind=kLoop, calls=%fused_computation | loop fusion | bytes 262148 | tf_op jit(solution)/shard_map/transpose | solution.py:318
  4.0 74.2 %shard_map.103 = (f32[4,30,16,256]{3,2,1,0:T(8,128)}, f32[4,30,16,256]{3,2,1,0:T(8,128)}, f32[8,16]{1,0:T(8,128)}) custom-call(bf16[30,128,128]{2,1,0:T(8,128)(2,1)} %act.1, bf16[4,64,256]{2,1,0:T(8,128)(2,1)} %dynamic-slice_bitcast_fusion.core, f32[30,30,30,30]{3,2,1,0:T(8,128)} %rdm.1, f32[30,30]{1,0:T(8,128)} %rot.1, s32[1]{0:T(128)S(6)} %copy.14.block, ...), custom_call_target="tpu_custom_call" | custom-call | tf_op jit(solution)/shard_map/pallas_call | solution.py:324
  78.2 0.0 copy-start
  78.2 4.2 %copy.11 = f32[16,30,4,256]{3,2,1,0:T(4,128)} copy(f32[16,30,4,256]{3,0,1,2:T(8,128)} %bitcast.10) | data formatting | bytes 3932160
  82.4 0.0 copy-done
  82.4 0.0 copy-start.1
  82.4 2.5 %copy.12 = f32[16,30,4,256]{3,2,1,0:T(4,128)} copy(f32[16,30,4,256]{3,0,1,2:T(8,128)S(1)} %bitcast.9) | data formatting | bytes 3932160
  85.0 0.0 copy-done.1
  85.0 0.6 copy.15
Async XLA Ops:
  78.2 4.2 %copy-start = (f32[4,30,16,256]{3,2,1,0:T(8,128)S(1)}, f32[4,30,16,256]{3,2,1,0:T(8,128)}, u32[]{:S(2)}) copy-start(f32[4,30,16,256]{3,2,1,0:T(8,128)} %get-tuple-element.7) | copy-start | bytes 5898244
  82.4 2.5 %copy-start.1 = (f32[8,16]{1,0:T(8,128)S(1)}, f32[8,16]{1,0:T(8,128)}, u32[]{:S(2)}) copy-start(f32[8,16]{1,0:T(8,128)} %get-tuple-element.8) | copy-start | bytes 1540

commit v2 on v1

v2 whole, which is shorter than its diff:
```python
import jax
import jax.numpy as jnp
from jax import lax
from jax.experimental import pallas as pl
from jax.experimental.pallas import tpu as pltpu
from jax.sharding import PartitionSpec as P

NBLK = 32
F32 = jnp.float32
BF16 = jnp.bfloat16
HIGH = lax.Precision.HIGHEST
NT = (((1,), (1,)), ((), ()))

ORDER = (
    ("A", 0, 0, 1), ("A", -1, 0, 0), ("A", 1, 0, 0), ("C", 0, -1, 0), ("C", 0, 1, 0), ("C", -1, 0, 0),
    ("C", 1, 0, 0), ("T", 0), ("T", 1), ("A", -1, 0, 1), ("A", 1, 0, 1), ("T", 2), ("T", 3), ("C", -1, -1, 0),
    ("C", 1, -1, 0), ("T", 4), ("G",), ("A", 0, -1, 0), ("A", 0, 1, 0), ("C", -1, 1, 0), ("C", 1, 1, 0),
    ("C", 0, -2, 0), ("C", 0, 2, 0), ("C", 2, 0, 0), ("C", 2, -1, 0), ("C", 2, 1, 0), ("A", -1, -1, 0),
    ("A", 1, -1, 0), ("M", 0, 0), ("A", 0, -1, 1), ("A", 0, 1, 1), ("M", 0, 1), ("C", -1, -2, 0),
    ("C", 1, -2, 0), ("A", -1, 1, 0), ("A", 1, 1, 0), ("C", 0, -3, 0), ("C", 0, 3, 0), ("C", -1, 2, 0),
    ("C", 1, 2, 0), ("C", 2, -2, 0), ("A", -1, -1, 1), ("A", 1, -1, 1), ("A", -1, 1, 1), ("A", 1, 1, 1),
    ("C", -1, -3, 0), ("C", 1, -3, 0), ("C", 0, 4, 0), ("C", -1, 3, 0), ("C", 1, 3, 0), ("C", 2, 2, 0),
    ("A", 0, 2, 0), ("M", "far", 0), ("C", 2, -3, 0), ("M", "far", 1), ("A", 0, 2, 1), ("C", -1, 4, 0),
    ("C", 1, 4, 0), ("A", -1, 2, 0), ("A", 1, 2, 0), ("C", 2, 3, 0), ("M", "near", 0), ("C", 2, 4, 0),
    ("M", "near", 1), ("A", -1, 2, 1), ("A", 1, 2, 1), ("M", 2, 0), ("M", 2, 1),
)

NEEDS = {
    0: ((0,), (0, 1, -1)),
    "far": ((1, -1), (1, -1, 2, -2)),
    "near": ((1, -1), (2, -2, 3, -3)),
    2: ((2,), (3, -3, 4)),
}


def kernel(
    act, slab, rdm, rot, block, levels, vir, occ,
    amp_one, amp_two, energy,
    abuf, cbuf, acc, slabv, core, rdmv, mix, tr, ebuf,
    send_sem, recv_a, recv_a2, recv_c, recv_c2, recv_e, local_sem,
):
    nact = act.shape[0]
    sub = abuf.shape[3]
    aux, row, col = lax.axis_index("aux"), lax.axis_index("row"), lax.axis_index("col")
    h, c = aux // 2, aux % 2
    z, y = h * 2 + row // 4, row % 4

    def device(dx=0, dy=0, dz=0, dc=0):
        zz = (z + dz + 8) % 8
        return (
            (zz // 2) * 2 + (c + dc) % 2,
            (zz % 2) * 4 + (y + dy + 4) % 4,
            (col + dx + 4) % 4,
        )

    def act_slot(dx, dh, dc):
        return (col + dx + 4) % 4, ((h + dh + 4) % 4) * 2 + (c + dc) % 2

    def core_slot(dy, dz, dc):
        a, r, _ = device(dy=dy, dz=dz, dc=dc)
        return a, r

    partners = [device(dz=2 * dh, dc=dc) for dh in range(4) for dc in range(2) if (dh, dc) != (0, 0)]
    partners += [device(dx=dx) for dx in (1, -1, 2)]
    partners += [device(dy=dy) for dy in (1, -1)]
    partners += [device(dz=dz) for dz in (1, -1)]
    barrier = pltpu.get_barrier_semaphore()
    for partner in partners:
        pl.semaphore_signal(barrier, inc=1, device_id=partner, device_id_type=pl.DeviceIdType.MESH)

    mine = act.at[:, pl.ds(pl.multiple_of(aux * sub, sub), sub), :]
    local = [
        pltpu.make_async_copy(slab, slabv, local_sem.at[0]),
        pltpu.make_async_copy(mine, abuf.at[col, aux], local_sem.at[1]),
        pltpu.make_async_copy(rdm, rdmv, local_sem.at[2]),
    ]
    for copy in local:
        copy.start()
    first_core = block[0] * core.shape[0]
    local[0].wait()
    for i in range(core.shape[0]):
        core[i] = slabv[first_core + i]
    pl.semaphore_wait(barrier, len(partners))

    sends = []

    def send(src, dst, sem, target):
        copy = pltpu.make_async_remote_copy(
            src_ref=src, dst_ref=dst, send_sem=send_sem.at[len(sends)], recv_sem=sem,
            device_id=target, device_id_type=pl.DeviceIdType.MESH,
        )
        copy.start()
        sends.append(copy)

    def arrived(dst, sem):
        pltpu.make_async_remote_copy(
            src_ref=dst, dst_ref=dst, send_sem=send_sem.at[0], recv_sem=sem,
            device_id=device(dc=1), device_id_type=pl.DeviceIdType.MESH,
        ).wait_recv()

    def scatter_act(dh, dc):
        target = device(dz=2 * dh, dc=dc)
        rows = pl.ds(pl.multiple_of(target[0] * sub, sub), sub)
        send(act.at[:, rows, :], abuf.at[col, aux], recv_a.at[col * 8 + aux], target)

    def pass_act(dx, dh, dc, to):
        x, j = act_slot(dx, dh, dc)
        send(abuf.at[x, j], abuf.at[x, j], recv_a.at[x * 8 + j], device(dx=to))

    def pass_core(from_y, from_z, **to):
        a, r = core_slot(from_y, from_z, 0)
        send(cbuf.at[a, r], cbuf.at[a, r], recv_c.at[a * 8 + r], device(**to))

    def part_act(dx, dh, dc, half, to):
        x, j = act_slot(dx, dh, dc)
        part = abuf.at[x, j, pl.ds(half * (nact // 2), nact // 2)]
        send(part, part, (recv_a2 if half else recv_a).at[x * 8 + j], device(dx=to))

    def part_core(from_y, from_z, half, **to):
        a, r = core_slot(from_y, from_z, 0)
        part = cbuf.at[a, r, pl.ds(2 * half, 2)]
        send(part, part, (recv_c2 if half else recv_c).at[a * 8 + r], device(**to))

    def on_act(dx, dh, dc):
        if dx == 0:
            pass_act(0, dh, dc, 1)
            pass_act(0, dh, dc, -1)
        if dx == -1:
            part_act(-1, dh, dc, 0, 1)
        if dx == 1:
            part_act(1, dh, dc, 1, -1)

    def on_core(dy, dz):
        if dy == 0:
            if -2 <= dz < 0:
                pass_core(0, dz, dz=1)
            if 0 < dz <= 2:
                pass_core(0, dz, dz=-1)
            if dz == -3:
                part_core(0, dz, 0, dz=1)
            if dz == 3:
                part_core(0, dz, 1, dz=-1)
            pass_core(0, dz, dy=1)
            pass_core(0, dz, dy=-1)
        if dy == -1:
            part_core(-1, dz, 0, dy=1)
        if dy == 1:
            part_core(1, dz, 1, dy=-1)
        pass_core(dy, dz, dc=1)
        if (dy, dz) == (0, 1):
            scatter_act(1, 1)
            scatter_act(-1, 1)
        if (dy, dz) == (0, 2):
            scatter_act(2, 0)
        if (dy, dz) == (0, 3):
            scatter_act(2, 1)

    for to in (dict(dz=1), dict(dz=-1), dict(dy=1), dict(dy=-1), dict(dc=1)):
        send(core, cbuf.at[aux, row], recv_c.at[aux * 8 + row], device(**to))
    scatter_act(1, 0)
    scatter_act(-1, 0)
    for to in (1, -1):
        send(mine, abuf.at[col, aux], recv_a.at[col * 8 + aux], device(dx=to))
    scatter_act(0, 1)
    cbuf[aux, row] = core[...]

    def trace_step(u, carry):
        by_lane = jnp.zeros((nact, nact), F32)
        by_row = jnp.zeros((nact, nact), F32)
        lanes = lax.broadcasted_iota(jnp.int32, (nact, nact), 1)
        rows = lax.broadcasted_iota(jnp.int32, (nact, nact), 0)
        for v in range(nact):
            piece = rdmv[u, v]
            by_lane = jnp.where(lanes == v, piece, by_lane)
            by_row = jnp.where(rows == v, piece, by_row)
        first = jnp.sum(by_lane, axis=1, keepdims=True)
        second = jnp.sum(by_row, axis=0, keepdims=True)
        tr[0] = jnp.where(lanes == u, first, tr[0])
        tr[1] = jnp.where(rows == u, second, tr[1])
        return carry

    def build_mix():
        eye = (
            lax.broadcasted_iota(jnp.int32, (nact, nact), 0) == lax.broadcasted_iota(jnp.int32, (nact, nact), 1)
        ).astype(F32)
        tall_row = lax.broadcasted_iota(jnp.int32, (256, nact), 0)
        tall_lane = lax.broadcasted_iota(jnp.int32, (256, nact), 1)
        by_orbital = (tall_row % 32 == tall_lane).astype(F32)
        spread = (tall_row // 8 == tall_lane).astype(F32)
        same = (
            lax.broadcasted_iota(jnp.int32, (256, 256), 0) // 32
            == lax.broadcasted_iota(jnp.int32, (256, 256), 1) % 8
        )

        def nt(a, b):
            return lax.dot_general(a, b, NT, precision=HIGH, preferred_element_type=F32)

        turn = rot[...]
        for k, small in enumerate((nt(nt(eye, tr[0]), turn), nt(tr[1], turn), nt(eye, turn))):
            tall = jnp.dot(by_orbital, small, precision=HIGH, preferred_element_type=F32)
            full = jnp.where(same, nt(tall, spread), 0.0)
            high = full.astype(BF16)
            low = (full - high.astype(F32)).astype(BF16)
            at = pl.ds(k * 256, 256)
            mix[at, 0:256] = high
            mix[at, 256:512] = low
            mix[at, 512:768] = high

    done = []

    def product(which, dc):
        low = row // 4
        away = {0: 0, 2: 2, "far": 2 * low - 1, "near": 1 - 2 * low}[which]
        j = ((h + away + 4) % 4) * 2 + (c + dc) % 2
        left = jnp.concatenate(
            [abuf[x, j].reshape(nact * sub, abuf.shape[4]) for x in range(4)], axis=1
        )
        first = not done
        done.append(j)

        for i in range(acc.shape[0]):
            right = cbuf[j, :, i].reshape(left.shape[1], cbuf.shape[4])
            out = jnp.dot(left, right, preferred_element_type=F32).reshape(acc.shape[1:])
            acc[i] = out if first else acc[i] + out

    waited = {("A", 0, 0, 0), ("C", 0, 0, 0)}

    def take(kind, *at):
        if (kind, *at) in waited:
            return
        waited.add((kind, *at))
        if kind == "A":
            x, j = act_slot(*at)
            if at[0] == 2:
                half = nact // 2
                arrived(abuf.at[x, j, pl.ds(0, half)], recv_a.at[x * 8 + j])
                arrived(abuf.at[x, j, pl.ds(half, half)], recv_a2.at[x * 8 + j])
            else:
                arrived(abuf.at[x, j], recv_a.at[x * 8 + j])
        else:
            a, r = core_slot(*at)
            if at[2] == 0 and (at[0] == 2 or at[1] == 4 and at[0] == 0):
                arrived(cbuf.at[a, r, pl.ds(0, 2)], recv_c.at[a * 8 + r])
                arrived(cbuf.at[a, r, pl.ds(2, 2)], recv_c2.at[a * 8 + r])
            else:
                arrived(cbuf.at[a, r], recv_c.at[a * 8 + r])

    for event in ORDER:
        kind = event[0]
        if kind == "A":
            take(*event)
            on_act(*event[1:])
        elif kind == "C":
            take(*event)
            on_core(event[1], event[2])
        elif kind == "T":
            part = event[1]
            if part == 0:
                local[2].wait()
                tr[...] = jnp.zeros_like(tr)
            lax.fori_loop(part * nact // 5, (part + 1) * nact // 5, trace_step, 0)
        elif kind == "G":
            build_mix()
        else:
            _, which, dc = event
            if not done:
                local[1].wait()
            for dh in NEEDS[which][0]:
                for dx in (0, 1, -1, 2):
                    take("A", dx, dh, dc)
            for dz in NEEDS[which][1]:
                for dy in (0, 1, -1, 2):
                    take("C", dy, dz, dc)
            product(which, dc)

    ebuf[col] = jnp.zeros(ebuf.shape[1:], F32)
    lanes = lax.broadcasted_iota(jnp.int32, (256, 128), 1)
    rows = lax.broadcasted_iota(jnp.int32, (256, 128), 0)
    vir_row = vir[pl.ds(row, 1), :]
    by_occ = jnp.sum(
        jnp.where(
            lax.broadcasted_iota(jnp.int32, (256, nact), 1)
            == lax.broadcasted_iota(jnp.int32, (256, nact), 0) % 32,
            occ[...],
            0.0,
        ),
        axis=1,
        keepdims=True,
    )
    by_col = jnp.concatenate([vir[pl.ds(2 * col, 1), :], vir[pl.ds(2 * col + 1, 1), :]], axis=1)
    slots = lax.broadcasted_iota(jnp.int32, (8, 128), 1)
    for g in range(2):
        at = pl.ds(8 * g, 8)
        by_row = by_occ + jnp.sum(
            jnp.where(lanes == aux * sub + g * 8 + rows // 32, vir_row, 0.0), axis=1, keepdims=True
        )

        def finish(i):
            tile = acc[i, :, at, :].reshape(8 * nact, acc.shape[3])
            high = tile.astype(BF16)
            low = (tile - high.astype(F32)).astype(BF16)
            pad = jnp.zeros((256 - 8 * nact, acc.shape[3]), BF16)
            right = jnp.concatenate([high, pad, high, pad, low, pad], axis=0)
            mixed = jnp.dot(mix[...], right, preferred_element_type=F32)
            scale = -1.0 / ((by_row - levels[first_core + i]) + by_col)
            turned = mixed[512:]
            for k, amp in enumerate((amp_one, amp_two)):
                value = mixed[256 * k : 256 * (k + 1)] * scale
                for half in range(2):
                    amp[pl.ds(g * 2048 + half * 4 + i, 256, stride=8), :] = value[:, 128 * half : 128 * (half + 1)]
                part = jnp.sum((value * turned).reshape(8, 32, acc.shape[3]), axis=1)
                part = jnp.sum(part, axis=1, keepdims=True)
                ebuf[col, at, :] = ebuf[col, at, :] + jnp.where(slots == k * 4 + i, part, 0.0)

        for i in range(acc.shape[0]):
            finish(i)
    for dx in (1, -1, 2):
        send(ebuf.at[col], ebuf.at[col], recv_e.at[col], device(dx=dx))
    for copy in sends[:-3]:
        copy.wait_send()
    for dx in (1, -1, 2):
        x = (col + dx + 4) % 4
        arrived(ebuf.at[x], recv_e.at[x])
    total = (((ebuf[0] + ebuf[1]) + ebuf[2]) + ebuf[3]).T
    energy[0] = total[:4]
    energy[1] = total[4:8]
    for copy in sends[-3:]:
        copy.wait_send()


def place(amp_one, amp_two, energy, one, two, out, sem):
    sub, nact, _, _ = one.shape
    copies = [pltpu.make_async_copy(energy, out, sem.at[4])]
    for k, (amp, to) in enumerate(((amp_one, one), (amp_two, two))):
        for half in range(2):
            copies.append(
                pltpu.make_async_copy(
                    amp.reshape(sub, 32, 8, 128).at[:, pl.ds(0, nact), pl.ds(4 * half, 4), :],
                    to.at[:, :, :, pl.ds(128 * half, 128)],
                    sem.at[2 * k + half],
                )
            )
    for copy in copies:
        copy.start()
    for copy in copies:
        copy.wait()


def shards(act_slab, core_slab, rotation, core_block, core_energy, vir_energy, act_energy, rdm_two):
    block_size = core_slab.shape[0] // NBLK
    nact, tile, depth = act_slab.shape
    sub = tile // lax.axis_size("aux")
    cols, core_depth = core_slab.shape[1:]
    slab = jnp.transpose(core_slab, (0, 2, 1))
    hbm = pl.BlockSpec(memory_space=pltpu.HBM)
    vmem = pl.BlockSpec(memory_space=pltpu.VMEM)
    smem = pl.BlockSpec(memory_space=pltpu.SMEM)
    mixed = pltpu.VMEM((sub * 32 * 2 * block_size, 128), F32)
    parts = pltpu.VMEM((2, block_size, sub), F32)
    amp_one, amp_two, energy = pl.pallas_call(
        kernel,
        out_shape=(mixed, mixed, parts),
        in_specs=[hbm, hbm, hbm, vmem, smem, smem, vmem, vmem],
        out_specs=(vmem, vmem, vmem),
        scratch_shapes=[
            pltpu.VMEM((4, 8, nact, sub, depth), BF16),
            pltpu.VMEM((8, 8, block_size, core_depth, cols), BF16),
            pltpu.VMEM((block_size, nact, sub, cols), F32),
            pltpu.VMEM(slab.shape, BF16),
            pltpu.VMEM((block_size, core_depth, cols), BF16),
            pltpu.VMEM(rdm_two.shape, F32),
            pltpu.VMEM((768, 768), BF16),
            pltpu.VMEM((2, nact, nact), F32),
            pltpu.VMEM((4, sub, 128), F32),
            pltpu.SemaphoreType.DMA((114,)),
            pltpu.SemaphoreType.DMA((32,)),
            pltpu.SemaphoreType.DMA((32,)),
            pltpu.SemaphoreType.DMA((64,)),
            pltpu.SemaphoreType.DMA((64,)),
            pltpu.SemaphoreType.DMA((4,)),
            pltpu.SemaphoreType.DMA((3,)),
        ],
        compiler_params=pltpu.CompilerParams(
            collective_id=0, has_side_effects=True, vmem_limit_bytes=56 * 2**20
        ),
    )(
        act_slab, slab, rdm_two, rotation, core_block, core_energy,
        vir_energy.reshape(8, 128), act_energy.reshape(1, nact),
    )
    out = jax.ShapeDtypeStruct((sub, nact, block_size, cols), F32)
    return tuple(
        pl.pallas_call(
            place,
            out_shape=(out, out, jax.ShapeDtypeStruct(parts.shape, F32)),
            in_specs=[vmem, vmem, vmem],
            out_specs=(hbm, hbm, hbm),
            scratch_shapes=[pltpu.SemaphoreType.DMA((5,))],
            compiler_params=pltpu.CompilerParams(vmem_limit_bytes=16 * 2**20),
        )(amp_one, amp_two, energy)
    )


def solution(mesh):
    in_specs = (
        P(None, "row", ("aux", "col")),
        P(None, "col", ("aux", "row")),
        P(),
        P(),
        P(),
        P(),
        P(),
        P(),
    )
    out_specs = (
        P(("row", "aux"), None, None, "col"),
        P(("row", "aux"), None, None, "col"),
        P(None, None, ("row", "aux")),
    )
    return jax.shard_map(shards, mesh=mesh, in_specs=in_specs, out_specs=out_specs, check_vma=False)
```

time: 85.7 us -> 67.4 us (0.79); the launches traced: 85.5 us -> 66.2 us
  local copies, waits for them, and re-layouts: 10.1 us -> 0 us
  Pallas kernels: 74.2 us -> 64.9 us
    pallas_call x1 -> x2, Pallas kernels: 74.2 us -> 64.9 us  [the longest x1 62.9 us: shards(): pl.pallas_call(kernel, out_shape=(mixed, mixed, parts), in_specs=[hbm, hb...]
    unnamed x7 -> x0, local copies, waits for them, and re-layouts: 7.36 us -> none
    transpose x1 -> x0, local copies, waits for them, and re-layouts: 1.57 us -> none  [shards(): core_rows = jnp.transpose(core_rows, (0, 2, 1))]
    reshape x1 -> x0, local copies, waits for them, and re-layouts: 1.17 us -> none  [shards(): occ = jnp.pad(act_energy, (0, 128 - nact)).reshape(1, 128)]
where the time goes in v2:
time: 67.4 us; the launch traced here: 66.2 us
  Pallas kernels  64.9 us (96%)
  between operations  1.29 us (2%)
    pallas_call x1, Pallas kernels, shards(): pl.pallas_call(kernel, out_shape=(mixed, mixed, parts), in_specs=[hbm, hb...  62.9 us
    pallas_call x1, Pallas kernels, shards(): pl.pallas_call(place, out_shape=(out, out, jax.ShapeDtypeStruct(parts.sha...  1.96 us

profile of v2, /device:TPU:1, one launch (start us, length us, event | category | flops | bytes accessed | tf_op | source)
XLA Modules:
  0.0 66.2 jit_solution(4292958165190971561)
XLA Ops:
  1.3 62.9 %shard_map.103 = (f32[4096,128]{1,0:T(8,128)S(1)}, f32[4096,128]{1,0:T(8,128)S(1)}, f32[2,4,16]{2,1,0:T(4,128)S(1)}) custom-call(bf16[30,128,128]{2,1,0:T(8,128)(2,1)} %act.1, bf16[128,64,256]{2,1,0:T(8,128)(2,1)} %bitcast.3, f32[30,30,30,30]{3,2,1,0:T(8,128)} %rdm.1, f32[30,30]{1,0:T(8,128)} %rot.1, s32[1]{0:T(128)S(6)} %copy.11.block, f32[128]{0:T(128)} %levels.1, ...), custom_call_target="tpu_custom_call" | custom-call | tf_op jit(solution)/shard_map/pallas_call | solution.py:360
  64.2 2.0 %shard_map.104 = (f32[16,30,4,256]{3,2,1,0:T(4,128)}, f32[16,30,4,256]{3,2,1,0:T(4,128)}, f32[2,4,16]{2,1,0:T(4,128)}) custom-call(f32[4096,128]{1,0:T(8,128)S(1)} %get-tuple-element.6.amp_one, f32[4096,128]{1,0:T(8,128)S(1)} %get-tuple-element.7.amp_two, f32[2,4,16]{2,1,0:T(4,128)S(1)} %get-tuple-element.8.energy), custom_call_target="tpu_custom_call" | custom-call | tf_op jit(solution)/shard_map/pallas_call | solution.py:392

commit v3 on v2

--- a/solution.py
+++ b/solution.py
@@ -12,18 +12,23 @@
 NT = (((1,), (1,)), ((), ()))
 
 ORDER = (
-    ("A", 0, 0, 1), ("A", -1, 0, 0), ("A", 1, 0, 0), ("C", 0, -1, 0), ("C", 0, 1, 0), ("C", -1, 0, 0),
-    ("C", 1, 0, 0), ("T", 0), ("T", 1), ("A", -1, 0, 1), ("A", 1, 0, 1), ("T", 2), ("T", 3), ("C", -1, -1, 0),
-    ("C", 1, -1, 0), ("T", 4), ("G",), ("A", 0, -1, 0), ("A", 0, 1, 0), ("C", -1, 1, 0), ("C", 1, 1, 0),
-    ("C", 0, -2, 0), ("C", 0, 2, 0), ("C", 2, 0, 0), ("C", 2, -1, 0), ("C", 2, 1, 0), ("A", -1, -1, 0),
-    ("A", 1, -1, 0), ("M", 0, 0), ("A", 0, -1, 1), ("A", 0, 1, 1), ("M", 0, 1), ("C", -1, -2, 0),
-    ("C", 1, -2, 0), ("A", -1, 1, 0), ("A", 1, 1, 0), ("C", 0, -3, 0), ("C", 0, 3, 0), ("C", -1, 2, 0),
-    ("C", 1, 2, 0), ("C", 2, -2, 0), ("A", -1, -1, 1), ("A", 1, -1, 1), ("A", -1, 1, 1), ("A", 1, 1, 1),
-    ("C", -1, -3, 0), ("C", 1, -3, 0), ("C", 0, 4, 0), ("C", -1, 3, 0), ("C", 1, 3, 0), ("C", 2, 2, 0),
-    ("A", 0, 2, 0), ("M", "far", 0), ("C", 2, -3, 0), ("M", "far", 1), ("A", 0, 2, 1), ("C", -1, 4, 0),
-    ("C", 1, 4, 0), ("A", -1, 2, 0), ("A", 1, 2, 0), ("C", 2, 3, 0), ("M", "near", 0), ("C", 2, 4, 0),
-    ("M", "near", 1), ("A", -1, 2, 1), ("A", 1, 2, 1), ("M", 2, 0), ("M", 2, 1),
+    ("A", 0, 0, 1), ("A", -1, 0, 0), ("A", 1, 0, 0), ("C", 0, -1, 0), ("C", 0, 1, 0), ("S", 1, 1),
+    ("S", -1, 1), ("C", -1, 0, 0), ("C", 1, 0, 0), ("T", 0), ("T", 1), ("A", -1, 0, 1), ("A", 1, 0, 1),
+    ("T", 2), ("T", 3), ("C", -1, -1, 0), ("C", 1, -1, 0), ("T", 4), ("G",), ("A", 0, -1, 0), ("A", 0, 1, 0),
+    ("C", -1, 1, 0), ("C", 1, 1, 0), ("C", 0, -2, 0), ("C", 0, 2, 0), ("S", 2, 0), ("C", 2, -1, 0),
+    ("C", 2, 0, 0), ("A", -1, -1, 0), ("A", 1, -1, 0), ("C", -1, -2, 0), ("C", 2, 1, 0), ("A", -1, 1, 0),
+    ("A", 1, 1, 0), ("M", 0, 0), ("A", 0, -1, 1), ("A", 0, 1, 1), ("M", 0, 1), ("C", -1, 2, 0),
+    ("C", 1, -2, 0), ("C", 0, -3, 0), ("C", 0, 3, 0), ("C", 2, -2, 0), ("C", 1, 2, 0), ("S", 2, 1),
+    ("A", -1, -1, 1), ("A", 1, -1, 1), ("A", -1, 1, 1), ("C", 2, 2, 0), ("C", 1, -3, 0), ("C", 0, 4, 0),
+    ("M", "far", 0), ("A", 1, 1, 1), ("C", -1, -3, 0), ("C", 1, 3, 0), ("A", 0, 2, 0), ("M", "far", 1),
+    ("C", -1, 3, 0), ("C", 2, -3, 0), ("A", 0, 2, 1), ("A", -1, 2, 0), ("A", 1, 2, 0), ("C", -1, 4, 0),
+    ("C", 1, 4, 0), ("C", 2, 3, 0), ("M", "near", 0), ("A", -1, 2, 1), ("A", 1, 2, 1), ("M", "near", 1),
+    ("C", 2, 4, 0), ("M", 2, 0), ("M", 2, 1),
 )
+
+FIRST = ((1, 0), (-1, 0), (0, 1))
+
+SIDE = {('C', 1): 1, ('A', 0, 0): 1, ('A', 0, 1): 1, ('A', 1, 1): -1, ('C', 0): 1, ('A', 1, 0): 1, ('C', 4): 1, ('A', -1, 1): 1, ('C', -3): 1, ('C', 2): -1, ('A', -1, 0): -1, ('C', -2): -1, ('C', -1): -1}
 
 NEEDS = {
     0: ((0,), (0, 1, -1)),
@@ -34,31 +39,32 @@
 
 
 def kernel(
-    act, slab, rdm, rot, block, levels, vir, occ,
+    act, slab, rdm, rot, block, levels, vir_one, vir, occ,
     amp_one, amp_two, energy,
-    abuf, cbuf, acc, slabv, core, rdmv, mix, tr, ebuf,
+    abuf, cbuf, acc, slabv, core, rdmv, mix, tr, parts, ebuf,
     send_sem, recv_a, recv_a2, recv_c, recv_c2, recv_e, local_sem,
 ):
     nact = act.shape[0]
     sub = abuf.shape[3]
     aux, row, col = lax.axis_index("aux"), lax.axis_index("row"), lax.axis_index("col")
-    h, c = aux // 2, aux % 2
-    z, y = h * 2 + row // 4, row % 4
+    h, c = lax.div(aux, 2), lax.rem(aux, 2)
+    z, y = h * 2 + lax.div(row, 4), lax.rem(row, 4)
+    column = [lax.rem(col + dx, 4) for dx in range(4)]
+    line = [lax.rem(y + dy, 4) for dy in range(4)]
+    core_id = [c, 1 - c]
+    level_of = [lax.rem(z + dz, 8) for dz in range(8)]
+    group = [[lax.div(zz, 2) * 2 + core_id[dc] for dc in range(2)] for zz in level_of]
+    layer = [lax.rem(zz, 2) for zz in level_of]
+    rows_of = [[low * 4 + line[dy] for dy in range(4)] for low in layer]
 
     def device(dx=0, dy=0, dz=0, dc=0):
-        zz = (z + dz + 8) % 8
-        return (
-            (zz // 2) * 2 + (c + dc) % 2,
-            (zz % 2) * 4 + (y + dy + 4) % 4,
-            (col + dx + 4) % 4,
-        )
+        return group[dz % 8][dc % 2], rows_of[dz % 8][dy % 4], column[dx % 4]
 
     def act_slot(dx, dh, dc):
-        return (col + dx + 4) % 4, ((h + dh + 4) % 4) * 2 + (c + dc) % 2
+        return column[dx % 4], group[2 * dh % 8][dc % 2]
 
     def core_slot(dy, dz, dc):
-        a, r, _ = device(dy=dy, dz=dz, dc=dc)
-        return a, r
+        return group[dz % 8][dc % 2], rows_of[dz % 8][dy % 4]
 
     partners = [device(dz=2 * dh, dc=dc) for dh in range(4) for dc in range(2) if (dh, dc) != (0, 0)]
     partners += [device(dx=dx) for dx in (1, -1, 2)]
@@ -125,10 +131,11 @@
         if dx == 0:
             pass_act(0, dh, dc, 1)
             pass_act(0, dh, dc, -1)
-        if dx == -1:
-            part_act(-1, dh, dc, 0, 1)
-        if dx == 1:
-            part_act(1, dh, dc, 1, -1)
+        side = SIDE.get(("A", dh, dc), 0)
+        if side == 0 and abs(dx) == 1:
+            part_act(dx, dh, dc, (dx + 1) // 2, -dx)
+        if side != 0 and dx == side:
+            pass_act(dx, dh, dc, -dx)
 
     def on_core(dy, dz):
         if dy == 0:
@@ -142,26 +149,19 @@
                 part_core(0, dz, 1, dz=-1)
             pass_core(0, dz, dy=1)
             pass_core(0, dz, dy=-1)
-        if dy == -1:
-            part_core(-1, dz, 0, dy=1)
-        if dy == 1:
-            part_core(1, dz, 1, dy=-1)
+        side = SIDE.get(("C", dz), 0)
+        if side == 0 and abs(dy) == 1:
+            part_core(dy, dz, (dy + 1) // 2, dy=-dy)
+        if side != 0 and dy == side:
+            pass_core(dy, dz, dy=-dy)
         pass_core(dy, dz, dc=1)
-        if (dy, dz) == (0, 1):
-            scatter_act(1, 1)
-            scatter_act(-1, 1)
-        if (dy, dz) == (0, 2):
-            scatter_act(2, 0)
-        if (dy, dz) == (0, 3):
-            scatter_act(2, 1)
 
     for to in (dict(dz=1), dict(dz=-1), dict(dy=1), dict(dy=-1), dict(dc=1)):
         send(core, cbuf.at[aux, row], recv_c.at[aux * 8 + row], device(**to))
-    scatter_act(1, 0)
-    scatter_act(-1, 0)
     for to in (1, -1):
         send(mine, abuf.at[col, aux], recv_a.at[col * 8 + aux], device(dx=to))
-    scatter_act(0, 1)
+    for event in FIRST:
+        scatter_act(*event)
     cbuf[aux, row] = core[...]
 
     def trace_step(u, carry):
@@ -183,28 +183,20 @@
         eye = (
             lax.broadcasted_iota(jnp.int32, (nact, nact), 0) == lax.broadcasted_iota(jnp.int32, (nact, nact), 1)
         ).astype(F32)
-        tall_row = lax.broadcasted_iota(jnp.int32, (256, nact), 0)
-        tall_lane = lax.broadcasted_iota(jnp.int32, (256, nact), 1)
-        by_orbital = (tall_row % 32 == tall_lane).astype(F32)
-        spread = (tall_row // 8 == tall_lane).astype(F32)
-        same = (
-            lax.broadcasted_iota(jnp.int32, (256, 256), 0) // 32
-            == lax.broadcasted_iota(jnp.int32, (256, 256), 1) % 8
-        )
+        padded = (
+            lax.broadcasted_iota(jnp.int32, (32, nact), 0) == lax.broadcasted_iota(jnp.int32, (32, nact), 1)
+        ).astype(F32)
 
         def nt(a, b):
             return lax.dot_general(a, b, NT, precision=HIGH, preferred_element_type=F32)
 
         turn = rot[...]
         for k, small in enumerate((nt(nt(eye, tr[0]), turn), nt(tr[1], turn), nt(eye, turn))):
-            tall = jnp.dot(by_orbital, small, precision=HIGH, preferred_element_type=F32)
-            full = jnp.where(same, nt(tall, spread), 0.0)
+            tall = jnp.dot(padded, small, precision=HIGH, preferred_element_type=F32)
+            full = nt(tall, padded)
             high = full.astype(BF16)
             low = (full - high.astype(F32)).astype(BF16)
-            at = pl.ds(k * 256, 256)
-            mix[at, 0:256] = high
-            mix[at, 256:512] = low
-            mix[at, 512:768] = high
+            mix[pl.ds(32 * k, 32), :] = jnp.concatenate([high, low, high, jnp.zeros_like(high)], axis=1)
 
     done = []
 
@@ -218,10 +210,13 @@
         first = not done
         done.append(j)
 
-        for i in range(acc.shape[0]):
+        for i in range(cbuf.shape[2]):
             right = cbuf[j, :, i].reshape(left.shape[1], cbuf.shape[4])
-            out = jnp.dot(left, right, preferred_element_type=F32).reshape(acc.shape[1:])
-            acc[i] = out if first else acc[i] + out
+            out = jnp.dot(left, right, preferred_element_type=F32)
+            for half in range(2):
+                at = (2 * i + half, pl.ds(0, nact * sub))
+                part = out[:, 128 * half : 128 * (half + 1)]
+                acc[at] = part if first else acc[at] + part
 
     waited = {("A", 0, 0, 0), ("C", 0, 0, 0)}
 
@@ -231,7 +226,7 @@
         waited.add((kind, *at))
         if kind == "A":
             x, j = act_slot(*at)
-            if at[0] == 2:
+            if at[0] == 2 and ("A", *at[1:]) not in SIDE:
                 half = nact // 2
                 arrived(abuf.at[x, j, pl.ds(0, half)], recv_a.at[x * 8 + j])
                 arrived(abuf.at[x, j, pl.ds(half, half)], recv_a2.at[x * 8 + j])
@@ -239,7 +234,8 @@
                 arrived(abuf.at[x, j], recv_a.at[x * 8 + j])
         else:
             a, r = core_slot(*at)
-            if at[2] == 0 and (at[0] == 2 or at[1] == 4 and at[0] == 0):
+            halved = at[0] == 2 and ("C", at[1]) not in SIDE or at[:2] == (0, 4)
+            if at[2] == 0 and halved:
                 arrived(cbuf.at[a, r, pl.ds(0, 2)], recv_c.at[a * 8 + r])
                 arrived(cbuf.at[a, r, pl.ds(2, 2)], recv_c2.at[a * 8 + r])
             else:
@@ -253,11 +249,15 @@
         elif kind == "C":
             take(*event)
             on_core(event[1], event[2])
+        elif kind == "S":
+            scatter_act(*event[1:])
         elif kind == "T":
             part = event[1]
             if part == 0:
                 local[2].wait()
                 tr[...] = jnp.zeros_like(tr)
+                rest = pl.ds(nact * sub, (32 - nact) * sub)
+                acc[:, rest, :] = jnp.zeros((acc.shape[0], (32 - nact) * sub, 128), F32)
             lax.fori_loop(part * nact // 5, (part + 1) * nact // 5, trace_step, 0)
         elif kind == "G":
             build_mix()
@@ -273,47 +273,42 @@
                     take("C", dy, dz, dc)
             product(which, dc)
 
-    ebuf[col] = jnp.zeros(ebuf.shape[1:], F32)
-    lanes = lax.broadcasted_iota(jnp.int32, (256, 128), 1)
-    rows = lax.broadcasted_iota(jnp.int32, (256, 128), 0)
-    vir_row = vir[pl.ds(row, 1), :]
     by_occ = jnp.sum(
         jnp.where(
-            lax.broadcasted_iota(jnp.int32, (256, nact), 1)
-            == lax.broadcasted_iota(jnp.int32, (256, nact), 0) % 32,
+            lax.broadcasted_iota(jnp.int32, (32, nact), 1) == lax.broadcasted_iota(jnp.int32, (32, nact), 0),
             occ[...],
             0.0,
         ),
         axis=1,
         keepdims=True,
     )
-    by_col = jnp.concatenate([vir[pl.ds(2 * col, 1), :], vir[pl.ds(2 * col + 1, 1), :]], axis=1)
-    slots = lax.broadcasted_iota(jnp.int32, (8, 128), 1)
-    for g in range(2):
-        at = pl.ds(8 * g, 8)
-        by_row = by_occ + jnp.sum(
-            jnp.where(lanes == aux * sub + g * 8 + rows // 32, vir_row, 0.0), axis=1, keepdims=True
+    by_both = by_occ + jnp.concatenate([vir[pl.ds(2 * col, 1), :], vir[pl.ds(2 * col + 1, 1), :]], axis=1)
+    count = core.shape[0]
+    level = [levels[first_core + i] for i in range(count)]
+    for a in range(sub):
+        tile = jnp.concatenate(
+            [acc[n, pl.ds(a, 32, stride=sub), :] for n in range(acc.shape[0])], axis=1
         )
-
-        def finish(i):
-            tile = acc[i, :, at, :].reshape(8 * nact, acc.shape[3])
-            high = tile.astype(BF16)
-            low = (tile - high.astype(F32)).astype(BF16)
-            pad = jnp.zeros((256 - 8 * nact, acc.shape[3]), BF16)
-            right = jnp.concatenate([high, pad, high, pad, low, pad], axis=0)
-            mixed = jnp.dot(mix[...], right, preferred_element_type=F32)
-            scale = -1.0 / ((by_row - levels[first_core + i]) + by_col)
-            turned = mixed[512:]
+        high = tile.astype(BF16)
+        low = (tile - high.astype(F32)).astype(BF16)
+        right = jnp.concatenate([high, high, low, jnp.zeros_like(high)], axis=0)
+        mixed = jnp.dot(mix[...], right, preferred_element_type=F32)
+        own = vir_one[row * 128 + aux * sub + a]
+        for i in range(count):
+            at = slice(256 * i, 256 * (i + 1))
+            scale = -1.0 / (by_both + (own - level[i]))
+            turned = mixed[64:96, at]
             for k, amp in enumerate((amp_one, amp_two)):
-                value = mixed[256 * k : 256 * (k + 1)] * scale
+                value = mixed[32 * k : 32 * (k + 1), at] * scale
                 for half in range(2):
-                    amp[pl.ds(g * 2048 + half * 4 + i, 256, stride=8), :] = value[:, 128 * half : 128 * (half + 1)]
-                part = jnp.sum((value * turned).reshape(8, 32, acc.shape[3]), axis=1)
-                part = jnp.sum(part, axis=1, keepdims=True)
-                ebuf[col, at, :] = ebuf[col, at, :] + jnp.where(slots == k * 4 + i, part, 0.0)
-
-        for i in range(acc.shape[0]):
-            finish(i)
+                    amp[pl.ds(a * 256 + half * 4 + i, 32, stride=8), :] = value[:, 128 * half : 128 * (half + 1)]
+                part = value * turned
+                part = (part[:, :128] + part[:, 128:]).reshape(4, 8, 128)
+                parts[(k * count + i) * sub + a] = (part[0] + part[1]) + (part[2] + part[3])
+    summed = jnp.sum(jnp.sum(parts[...], axis=1), axis=1, keepdims=True)
+    here = lax.broadcasted_iota(jnp.int32, (2 * count * sub, 128), 0) % sub
+    spot = here == lax.broadcasted_iota(jnp.int32, (2 * count * sub, 128), 1)
+    ebuf[col] = jnp.sum(jnp.where(spot, summed, 0.0).reshape(2 * count, sub, 128), axis=1)
     for dx in (1, -1, 2):
         send(ebuf.at[col], ebuf.at[col], recv_e.at[col], device(dx=dx))
     for copy in sends[:-3]:
@@ -321,9 +316,9 @@
     for dx in (1, -1, 2):
         x = (col + dx + 4) % 4
         arrived(ebuf.at[x], recv_e.at[x])
-    total = (((ebuf[0] + ebuf[1]) + ebuf[2]) + ebuf[3]).T
-    energy[0] = total[:4]
-    energy[1] = total[4:8]
+    total = ((ebuf[0] + ebuf[1]) + ebuf[2]) + ebuf[3]
+    energy[0] = total[:count, :sub]
+    energy[1] = total[count:, :sub]
     for copy in sends[-3:]:
         copy.wait_send()
 
@@ -360,18 +355,19 @@
     amp_one, amp_two, energy = pl.pallas_call(
         kernel,
         out_shape=(mixed, mixed, parts),
-        in_specs=[hbm, hbm, hbm, vmem, smem, smem, vmem, vmem],
+        in_specs=[hbm, hbm, hbm, vmem, smem, smem, smem, vmem, vmem],
         out_specs=(vmem, vmem, vmem),
         scratch_shapes=[
             pltpu.VMEM((4, 8, nact, sub, depth), BF16),
             pltpu.VMEM((8, 8, block_size, core_depth, cols), BF16),
-            pltpu.VMEM((block_size, nact, sub, cols), F32),
+            pltpu.VMEM((2 * block_size, 32 * sub, 128), F32),
             pltpu.VMEM(slab.shape, BF16),
             pltpu.VMEM((block_size, core_depth, cols), BF16),
             pltpu.VMEM(rdm_two.shape, F32),
-            pltpu.VMEM((768, 768), BF16),
+            pltpu.VMEM((96, 128), BF16),
             pltpu.VMEM((2, nact, nact), F32),
-            pltpu.VMEM((4, sub, 128), F32),
+            pltpu.VMEM((2 * block_size * sub, 8, 128), F32),
+            pltpu.VMEM((4, 2 * block_size, 128), F32),
             pltpu.SemaphoreType.DMA((114,)),
             pltpu.SemaphoreType.DMA((32,)),
             pltpu.SemaphoreType.DMA((32,)),
@@ -385,7 +381,7 @@
         ),
     )(
         act_slab, slab, rdm_two, rotation, core_block, core_energy,
-        vir_energy.reshape(8, 128), act_energy.reshape(1, nact),
+        vir_energy, vir_energy.reshape(8, 128), act_energy.reshape(1, nact),
     )
     out = jax.ShapeDtypeStruct((sub, nact, block_size, cols), F32)
     return tuple(

time: 67.4 us -> 65.6 us (0.973); the launches traced: 66.2 us -> 65.3 us
  Pallas kernels: 64.9 us -> 64 us
    pallas_call x1, Pallas kernels: 62.9 us -> 62 us  [shards(): pl.pallas_call(kernel, out_shape=(mixed, mixed, parts), in_specs=[hbm, hb...]
where the time goes in v3:
time: 65.6 us; the launch traced here: 65.3 us
  Pallas kernels  64 us (98%)
  between operations  1.29 us (2%)
    pallas_call x1, Pallas kernels, shards(): pl.pallas_call(kernel, out_shape=(mixed, mixed, parts), in_specs=[hbm, hb...  62 us
    pallas_call x1, Pallas kernels, shards(): pl.pallas_call(place, out_shape=(out, out, jax.ShapeDtypeStruct(parts.sha...  1.96 us

profile of v3, /device:TPU:1, one launch (start us, length us, event | category | flops | bytes accessed | tf_op | source)
XLA Modules:
  0.0 65.3 jit_solution(3769595788664302160)
XLA Ops:
  1.3 62.0 %shard_map.103 = (f32[4096,128]{1,0:T(8,128)S(1)}, f32[4096,128]{1,0:T(8,128)S(1)}, f32[2,4,16]{2,1,0:T(4,128)S(1)}) custom-call(bf16[30,128,128]{2,1,0:T(8,128)(2,1)} %act.1, bf16[128,64,256]{2,1,0:T(8,128)(2,1)} %bitcast.3, f32[30,30,30,30]{3,2,1,0:T(8,128)} %rdm.1, f32[30,30]{1,0:T(8,128)} %rot.1, s32[1]{0:T(128)S(6)} %copy.11.block, f32[128]{0:T(128)} %levels.1, ...), custom_call_target="tpu_custom_call" | custom-call | tf_op jit(solution)/shard_map/pallas_call | solution.py:355
  63.3 2.0 %shard_map.104 = (f32[16,30,4,256]{3,2,1,0:T(4,128)}, f32[16,30,4,256]{3,2,1,0:T(4,128)}, f32[2,4,16]{2,1,0:T(4,128)}) custom-call(f32[4096,128]{1,0:T(8,128)S(1)} %get-tuple-element.6.amp_one, f32[4096,128]{1,0:T(8,128)S(1)} %get-tuple-element.7.amp_two, f32[2,4,16]{2,1,0:T(4,128)S(1)} %get-tuple-element.8.energy), custom_call_target="tpu_custom_call" | custom-call | tf_op jit(solution)/shard_map/pallas_call | solution.py:388

commit v4 on v3

--- a/solution.py
+++ b/solution.py
@@ -285,24 +285,26 @@
     by_both = by_occ + jnp.concatenate([vir[pl.ds(2 * col, 1), :], vir[pl.ds(2 * col + 1, 1), :]], axis=1)
     count = core.shape[0]
     level = [levels[first_core + i] for i in range(count)]
-    for a in range(sub):
+    def mixes(a):
         tile = jnp.concatenate(
             [acc[n, pl.ds(a, 32, stride=sub), :] for n in range(acc.shape[0])], axis=1
         )
         high = tile.astype(BF16)
         low = (tile - high.astype(F32)).astype(BF16)
         right = jnp.concatenate([high, high, low, jnp.zeros_like(high)], axis=0)
-        mixed = jnp.dot(mix[...], right, preferred_element_type=F32)
+        return jnp.dot(mix[...], right, preferred_element_type=F32)
+
+    def scales(a, i):
         own = vir_one[row * 128 + aux * sub + a]
+        return -1.0 / (by_both + (own - level[i]))
+
+    for a in range(sub):
+        mixed = mixes(a)
         for i in range(count):
             at = slice(256 * i, 256 * (i + 1))
-            scale = -1.0 / (by_both + (own - level[i]))
-            turned = mixed[64:96, at]
-            for k, amp in enumerate((amp_one, amp_two)):
-                value = mixed[32 * k : 32 * (k + 1), at] * scale
-                for half in range(2):
-                    amp[pl.ds(a * 256 + half * 4 + i, 32, stride=8), :] = value[:, 128 * half : 128 * (half + 1)]
-                part = value * turned
+            turned = mixed[64:96, at] * scales(a, i)
+            for k in range(2):
+                part = mixed[32 * k : 32 * (k + 1), at] * turned
                 part = (part[:, :128] + part[:, 128:]).reshape(4, 8, 128)
                 parts[(k * count + i) * sub + a] = (part[0] + part[1]) + (part[2] + part[3])
     summed = jnp.sum(jnp.sum(parts[...], axis=1), axis=1, keepdims=True)
@@ -311,6 +313,15 @@
     ebuf[col] = jnp.sum(jnp.where(spot, summed, 0.0).reshape(2 * count, sub, 128), axis=1)
     for dx in (1, -1, 2):
         send(ebuf.at[col], ebuf.at[col], recv_e.at[col], device(dx=dx))
+    for a in range(sub):
+        mixed = mixes(a)
+        for i in range(count):
+            at = slice(256 * i, 256 * (i + 1))
+            scale = scales(a, i)
+            for k, amp in enumerate((amp_one, amp_two)):
+                value = mixed[32 * k : 32 * (k + 1), at] * scale
+                for half in range(2):
+                    amp[pl.ds(a * 256 + half * 4 + i, 32, stride=8), :] = value[:, 128 * half : 128 * (half + 1)]
     for copy in sends[:-3]:
         copy.wait_send()
     for dx in (1, -1, 2):

time: 65.6 us -> 65.1 us (level)
  no operation moved by 1% of the time
where the time goes in v4:
time: 65.1 us; the launch traced here: 64.8 us
  Pallas kernels  63.5 us (98%)
  between operations  1.29 us (2%)
    pallas_call x1, Pallas kernels, shards(): pl.pallas_call(kernel, out_shape=(mixed, mixed, parts), in_specs=[hbm, hb...  61.6 us
    pallas_call x1, Pallas kernels, shards(): pl.pallas_call(place, out_shape=(out, out, jax.ShapeDtypeStruct(parts.sha...  1.96 us

profile of v4, /device:TPU:1, one launch (start us, length us, event | category | flops | bytes accessed | tf_op | source)
XLA Modules:
  0.0 64.8 jit_solution(16465309443708689218)
XLA Ops:
  1.3 61.6 %shard_map.103 = (f32[4096,128]{1,0:T(8,128)S(1)}, f32[4096,128]{1,0:T(8,128)S(1)}, f32[2,4,16]{2,1,0:T(4,128)S(1)}) custom-call(bf16[30,128,128]{2,1,0:T(8,128)(2,1)} %act.1, bf16[128,64,256]{2,1,0:T(8,128)(2,1)} %bitcast.3, f32[30,30,30,30]{3,2,1,0:T(8,128)} %rdm.1, f32[30,30]{1,0:T(8,128)} %rot.1, s32[1]{0:T(128)S(6)} %copy.11.block, f32[128]{0:T(128)} %levels.1, ...), custom_call_target="tpu_custom_call" | custom-call | tf_op jit(solution)/shard_map/pallas_call | solution.py:366
  62.8 2.0 %shard_map.104 = (f32[16,30,4,256]{3,2,1,0:T(4,128)}, f32[16,30,4,256]{3,2,1,0:T(4,128)}, f32[2,4,16]{2,1,0:T(4,128)}) custom-call(f32[4096,128]{1,0:T(8,128)S(1)} %get-tuple-element.6.amp_one, f32[4096,128]{1,0:T(8,128)S(1)} %get-tuple-element.7.amp_two, f32[2,4,16]{2,1,0:T(4,128)S(1)} %get-tuple-element.8.energy), custom_call_target="tpu_custom_call" | custom-call | tf_op jit(solution)/shard_map/pallas_call | solution.py:399

commit v5 on v4

--- a/solution.py
+++ b/solution.py
@@ -41,7 +41,7 @@
 def kernel(
     act, slab, rdm, rot, block, levels, vir_one, vir, occ,
     amp_one, amp_two, energy,
-    abuf, cbuf, acc, slabv, core, rdmv, mix, tr, parts, ebuf,
+    abuf, cbuf, acc, slabv, core, rdmv, mix, scales, tr, parts, ebuf,
     send_sem, recv_a, recv_a2, recv_c, recv_c2, recv_e, local_sem,
 ):
     nact = act.shape[0]
@@ -241,6 +241,25 @@
             else:
                 arrived(cbuf.at[a, r], recv_c.at[a * 8 + r])
 
+    by_occ = jnp.sum(
+        jnp.where(
+            lax.broadcasted_iota(jnp.int32, (32, nact), 1) == lax.broadcasted_iota(jnp.int32, (32, nact), 0),
+            occ[...],
+            0.0,
+        ),
+        axis=1,
+        keepdims=True,
+    )
+    by_both = by_occ + jnp.concatenate([vir[pl.ds(2 * col, 1), :], vir[pl.ds(2 * col + 1, 1), :]], axis=1)
+    count = core.shape[0]
+    level = [levels[first_core + i] for i in range(count)]
+
+    def store_scales(a, carry):
+        own = vir_one[row * 128 + aux * sub + a]
+        for i in range(count):
+            scales[a, :, 256 * i : 256 * (i + 1)] = -1.0 / (by_both + (own - level[i]))
+        return carry
+
     for event in ORDER:
         kind = event[0]
         if kind == "A":
@@ -261,6 +280,7 @@
             lax.fori_loop(part * nact // 5, (part + 1) * nact // 5, trace_step, 0)
         elif kind == "G":
             build_mix()
+            lax.fori_loop(0, sub, store_scales, 0)
         else:
             _, which, dc = event
             if not done:
@@ -273,18 +293,6 @@
                     take("C", dy, dz, dc)
             product(which, dc)
 
-    by_occ = jnp.sum(
-        jnp.where(
-            lax.broadcasted_iota(jnp.int32, (32, nact), 1) == lax.broadcasted_iota(jnp.int32, (32, nact), 0),
-            occ[...],
-            0.0,
-        ),
-        axis=1,
-        keepdims=True,
-    )
-    by_both = by_occ + jnp.concatenate([vir[pl.ds(2 * col, 1), :], vir[pl.ds(2 * col + 1, 1), :]], axis=1)
-    count = core.shape[0]
-    level = [levels[first_core + i] for i in range(count)]
     def mixes(a):
         tile = jnp.concatenate(
             [acc[n, pl.ds(a, 32, stride=sub), :] for n in range(acc.shape[0])], axis=1
@@ -294,15 +302,11 @@
         right = jnp.concatenate([high, high, low, jnp.zeros_like(high)], axis=0)
         return jnp.dot(mix[...], right, preferred_element_type=F32)
 
-    def scales(a, i):
-        own = vir_one[row * 128 + aux * sub + a]
-        return -1.0 / (by_both + (own - level[i]))
-
     for a in range(sub):
         mixed = mixes(a)
         for i in range(count):
             at = slice(256 * i, 256 * (i + 1))
-            turned = mixed[64:96, at] * scales(a, i)
+            turned = mixed[64:96, at] * scales[a, :, at]
             for k in range(2):
                 part = mixed[32 * k : 32 * (k + 1), at] * turned
                 part = (part[:, :128] + part[:, 128:]).reshape(4, 8, 128)
@@ -317,7 +321,7 @@
         mixed = mixes(a)
         for i in range(count):
             at = slice(256 * i, 256 * (i + 1))
-            scale = scales(a, i)
+            scale = scales[a, :, at]
             for k, amp in enumerate((amp_one, amp_two)):
                 value = mixed[32 * k : 32 * (k + 1), at] * scale
                 for half in range(2):
@@ -376,6 +380,7 @@
             pltpu.VMEM((block_size, core_depth, cols), BF16),
             pltpu.VMEM(rdm_two.shape, F32),
             pltpu.VMEM((96, 128), BF16),
+            pltpu.VMEM((sub, 32, block_size * cols), F32),
             pltpu.VMEM((2, nact, nact), F32),
             pltpu.VMEM((2 * block_size * sub, 8, 128), F32),
             pltpu.VMEM((4, 2 * block_size, 128), F32),

time: 65.1 us -> 65.3 us (level)
  no operation moved by 1% of the time
where the time goes in v5:
time: 65.3 us; the launch traced here: 64.9 us
  Pallas kernels  63.6 us (97%)
  between operations  1.29 us (2%)
    pallas_call x1, Pallas kernels, shards(): pl.pallas_call(kernel, out_shape=(mixed, mixed, parts), in_specs=[hbm, hb...  61.7 us
    pallas_call x1, Pallas kernels, shards(): pl.pallas_call(place, out_shape=(out, out, jax.ShapeDtypeStruct(parts.sha...  1.96 us

profile of v5, /device:TPU:1, one launch (start us, length us, event | category | flops | bytes accessed | tf_op | source)
XLA Modules:
  0.0 64.9 jit_solution(10931128442903693518)
XLA Ops:
  1.3 61.7 %shard_map.103 = (f32[4096,128]{1,0:T(8,128)S(1)}, f32[4096,128]{1,0:T(8,128)S(1)}, f32[2,4,16]{2,1,0:T(4,128)S(1)}) custom-call(bf16[30,128,128]{2,1,0:T(8,128)(2,1)} %act.1, bf16[128,64,256]{2,1,0:T(8,128)(2,1)} %bitcast.3, f32[30,30,30,30]{3,2,1,0:T(8,128)} %rdm.1, f32[30,30]{1,0:T(8,128)} %rot.1, s32[1]{0:T(128)S(6)} %copy.11.block, f32[128]{0:T(128)} %levels.1, ...), custom_call_target="tpu_custom_call" | custom-call | tf_op jit(solution)/shard_map/pallas_call | solution.py:370
  63.0 2.0 %shard_map.104 = (f32[16,30,4,256]{3,2,1,0:T(4,128)}, f32[16,30,4,256]{3,2,1,0:T(4,128)}, f32[2,4,16]{2,1,0:T(4,128)}) custom-call(f32[4096,128]{1,0:T(8,128)S(1)} %get-tuple-element.6.amp_one, f32[4096,128]{1,0:T(8,128)S(1)} %get-tuple-element.7.amp_two, f32[2,4,16]{2,1,0:T(4,128)S(1)} %get-tuple-element.8.energy), custom_call_target="tpu_custom_call" | custom-call | tf_op jit(solution)/shard_map/pallas_call | solution.py:404
